TPU v7x, 32 devices: a whole 2x2x4 slice. The times are simulated.
32 devices in a mesh: fsdp: 8 (over z, core), seq: 4 (over y, x).
Axes of the slice: x: 2, y: 2, z: 4, core: 2. Of those that a mesh axis runs over, the one named last changes fastest.
Arguments:
- query_proj: bfloat16 [8, 512, 128], P('fsdp', 'seq'), may hold values from -6 to 6
- key_proj: bfloat16 [8, 512, 128], P('fsdp', 'seq'), may hold values from 0 to 5
- value_proj: bfloat16 [8, 512, 128], P('fsdp', 'seq'), may hold values from 0 to 5
- filters: float32 [128, 128], P('fsdp'), may hold values from -8 to 8
Outputs:
- response: bfloat16 [8, 512, 128], P('fsdp', 'seq')
All inputs are finite; a program needn't handle non-finite values.
Results may differ from a plain program's by a relative error of at most 0.012.
Values may be sent and summed in bfloat16 or wider, within the bound.
A program may use at most 64 MiB of HBM per device.

v0:
```python
import functools

import jax
import jax.numpy as jnp
from jax import lax
from jax.experimental import pallas as pl
from jax.experimental.pallas import tpu as pltpu
from jax.sharding import PartitionSpec as P

MESH = pl.DeviceIdType.MESH
LANES = 128
SUB = 8


def kernel(nf, ns, q_hbm, k_hbm, v_hbm, f_hbm, out_ref, kb, vb, qb, mix, halo, taps, tapsT, pad,
           load_sem, tail_send, tail_recv, f_send, f_recv):
    fi = lax.axis_index("fsdp")
    si = lax.axis_index("seq")
    span, channels = kb.shape
    own, width = f_hbm.shape
    halo_rows = halo.shape[0]
    mine = pl.ds(pl.multiple_of(fi * own, own), own)

    load_f = pltpu.make_async_copy(f_hbm, taps.at[mine], load_sem.at[0])
    load_k = pltpu.make_async_copy(k_hbm.at[0], kb, load_sem.at[1])
    load_v = pltpu.make_async_copy(v_hbm.at[0], vb, load_sem.at[2])
    load_q = pltpu.make_async_copy(q_hbm.at[0], qb, load_sem.at[3])
    load_f.start()
    load_k.start()
    load_v.start()
    load_q.start()

    barrier = pltpu.get_barrier_semaphore()
    for step in range(1, nf):
        pl.semaphore_signal(barrier, inc=1, device_id=(lax.rem(fi + step, nf), si), device_id_type=MESH)

    @pl.when(si > 0)
    def _():
        pl.semaphore_signal(barrier, inc=1, device_id=(fi, si - 1), device_id_type=MESH)

    load_k.wait()
    load_v.wait()
    mix[...] = (kb[...].astype(jnp.float32) * vb[...].astype(jnp.float32)).astype(jnp.bfloat16)
    for c in range(channels // LANES):
        pad[c, halo_rows:, :] = mix[:, c * LANES:(c + 1) * LANES].astype(jnp.float32)
    load_f.wait()

    @pl.when(si < ns - 1)
    def _():
        pl.semaphore_wait(barrier, nf)

    @pl.when(si == ns - 1)
    def _():
        pl.semaphore_wait(barrier, nf - 1)

    sends = []
    for step in range(1, nf):
        copy = pltpu.make_async_remote_copy(
            src_ref=taps.at[mine], dst_ref=taps.at[mine], send_sem=f_send, recv_sem=f_recv,
            device_id=(lax.rem(fi + step, nf), si), device_id_type=MESH)
        copy.start()
        sends.append(copy)
    tail = pltpu.make_async_remote_copy(
        src_ref=mix.at[pl.ds(span - halo_rows, halo_rows)], dst_ref=halo, send_sem=tail_send, recv_sem=tail_recv,
        device_id=(fi, lax.rem(si + 1, ns)), device_id_type=MESH)

    @pl.when(si < ns - 1)
    def _():
        tail.start()

    load_q.wait()

    @pl.when(si > 0)
    def _():
        tail.wait_recv()
        for c in range(channels // LANES):
            pad[c, :halo_rows, :] = halo[:, c * LANES:(c + 1) * LANES].astype(jnp.float32)

    @pl.when(si == 0)
    def _():
        for c in range(channels // LANES):
            pad[c, :halo_rows, :] = jnp.zeros((halo_rows, LANES), jnp.float32)

    others = taps.at[pl.ds(0, channels - own)]
    pltpu.make_async_copy(others, others, f_recv).wait()

    groups = width // SUB
    tiles = span // SUB
    base = halo_rows // SUB
    for c in range(channels // LANES):
        tapsT[...] = taps[c * LANES:(c + 1) * LANES, :].T

        def phase(b, acc):
            acc = list(acc)
            weights = [jnp.broadcast_to(tapsT[pl.ds(a * SUB + b, 1), :], (SUB, LANES)) for a in range(groups)]
            for row in range(base - groups + 1, base + tiles):
                window = pad[c, pl.ds(row * SUB - b, SUB), :]
                for a in range(groups):
                    j = row - base + a
                    if 0 <= j < tiles:
                        acc[j] = acc[j] + weights[a] * window
            return tuple(acc)

        acc = lax.fori_loop(0, SUB, phase, tuple(jnp.zeros((SUB, LANES), jnp.float32) for _ in range(tiles)))
        cols = slice(c * LANES, (c + 1) * LANES)
        gate = qb[:, cols].astype(jnp.float32)
        out_ref[0, :, cols] = (gate * jnp.concatenate(acc, axis=0)).astype(jnp.bfloat16)

    pltpu.make_async_copy(others, others, f_send).wait()

    @pl.when(si < ns - 1)
    def _():
        tail.wait_send()


def solution(mesh):
    nf, ns = mesh.shape["fsdp"], mesh.shape["seq"]

    def per_device(query_proj, key_proj, value_proj, filters):
        _, span, channels = key_proj.shape
        own, width = filters.shape
        return pl.pallas_call(
            functools.partial(kernel, nf, ns),
            out_shape=jax.ShapeDtypeStruct(query_proj.shape, jnp.bfloat16),
            in_specs=[pl.BlockSpec(memory_space=pltpu.HBM)] * 4,
            out_specs=pl.BlockSpec(memory_space=pltpu.VMEM),
            scratch_shapes=[
                pltpu.VMEM((span, channels), jnp.bfloat16),
                pltpu.VMEM((span, channels), jnp.bfloat16),
                pltpu.VMEM((span, channels), jnp.bfloat16),
                pltpu.VMEM((span, channels), jnp.bfloat16),
                pltpu.VMEM((width, channels), jnp.bfloat16),
                pltpu.VMEM((channels, width), jnp.float32),
                pltpu.VMEM((width, LANES), jnp.float32),
                pltpu.VMEM((channels // LANES, width + span, LANES), jnp.float32),
                pltpu.SemaphoreType.DMA((4,)),
                pltpu.SemaphoreType.DMA,
                pltpu.SemaphoreType.DMA,
                pltpu.SemaphoreType.DMA,
                pltpu.SemaphoreType.DMA,
            ],
            compiler_params=pltpu.CompilerParams(collective_id=0, has_side_effects=True,
                                                 vmem_limit_bytes=40 * 1024 * 1024),
        )(*[pltpu.with_memory_space_constraint(x, pltpu.HBM) for x in (query_proj, key_proj, value_proj, filters)])

    in_specs = (P("fsdp", "seq", None),) * 3 + (P("fsdp", None),)
    return jax.shard_map(per_device, mesh=mesh, in_specs=in_specs, out_specs=P("fsdp", "seq", None), check_vma=False)
```

profile of v0, /device:TPU:0, one launch (start us, length us, event | category | flops | bytes accessed | tf_op | source)
XLA Modules:
  0.0 9.6 jit_solution(15293977864477200464)
XLA Ops:
  0.0 9.0 %shard_map.46 = bf16[1,128,128]{2,1,0:T(8,128)(2,1)S(1)} custom-call(bf16[1,128,128]{2,1,0:T(8,128)(2,1)} %q_hbm.1, bf16[1,128,128]{2,1,0:T(8,128)(2,1)} %k_hbm.1, bf16[1,128,128]{2,1,0:T(8,128)(2,1)} %v_hbm.1, f32[16,128]{1,0:T(8,128)} %f_hbm.1), custom_call_target="tpu_custom_call" | custom-call | tf_op jit(solution)/shard_map/pallas_call | solution.py:122
  9.0 0.6 %copy.6 = bf16[1,128,128]{2,1,0:T(8,128)(2,1)} copy(bf16[1,128,128]{2,1,0:T(8,128)(2,1)S(1)} %shard_map.46) | data formatting | bytes 65536
where the time goes:
time: 9.77 us; the launch traced here: 9.6 us
  Pallas kernels  8.97 us (92%)
  local copies, waits for them, and re-layouts  0.62 us (6%)
    pallas_call x1, Pallas kernels, per_device(): pl.pallas_call(functools.partial(kernel, nf, ns), out_shape=jax.ShapeDtyp...  8.97 us
    unnamed x1, local copies, waits for them, and re-layouts  0.62 us

commit v1 on v0

v1 whole, which is shorter than its diff:
```python
import functools

import jax
import jax.numpy as jnp
from jax import lax
from jax.experimental import pallas as pl
from jax.experimental.pallas import tpu as pltpu
from jax.sharding import PartitionSpec as P

MESH = pl.DeviceIdType.MESH
LANES = 128
SUB = 8


def partners(index, count):
    if count & (count - 1):
        return [lax.rem(index + step, count) for step in range(1, count)]
    found = []
    for mask in sorted(range(1, count), key=lambda mask: (-(mask // 2), mask)):
        other = index
        for bit in range(count.bit_length()):
            if mask >> bit & 1:
                other = other + (1 << bit) * (1 - 2 * (index // (1 << bit) % 2))
        found.append(other)
    return found


def kernel(nf, ns, group, q_hbm, k_hbm, v_hbm, f_hbm, out_ref, kb, vb, qb, fb, mix, halo, taps, tapsT, packed, gates,
           done, load_sem, tail_send, tail_recv, f_send, f_recv):
    fi = lax.axis_index("fsdp")
    si = lax.axis_index("seq")
    span, channels = kb.shape
    own, width = f_hbm.shape
    groups, _, _ = packed.shape
    parts = LANES // group
    rows = span // parts
    mine = pl.ds(pl.multiple_of(fi * own, own), own)
    my_group = fi * own // group

    peers = partners(fi, nf)

    barrier = pltpu.get_barrier_semaphore()
    for peer in peers:
        pl.semaphore_signal(barrier, inc=1, device_id=(peer, si), device_id_type=MESH)

    @pl.when(si > 0)
    def _():
        pl.semaphore_signal(barrier, inc=1, device_id=(fi, si - 1), device_id_type=MESH)

    load_f = pltpu.make_async_copy(f_hbm, fb, load_sem.at[0])
    load_k = pltpu.make_async_copy(k_hbm.at[0], kb, load_sem.at[1])
    load_v = pltpu.make_async_copy(v_hbm.at[0], vb, load_sem.at[2])
    load_q = pltpu.make_async_copy(q_hbm.at[0], qb, load_sem.at[3])
    load_f.start()
    load_k.start()
    load_v.start()
    load_q.start()
    pltpu.make_async_copy(f_hbm, taps.at[mine], f_recv.at[my_group]).start()

    load_k.wait()
    load_v.wait()
    mix[...] = (kb[...].astype(jnp.float32) * vb[...].astype(jnp.float32)).astype(jnp.bfloat16)
    load_f.wait()

    @pl.when(si < ns - 1)
    def _():
        pl.semaphore_wait(barrier, nf)

    @pl.when(si == ns - 1)
    def _():
        pl.semaphore_wait(barrier, nf - 1)

    for peer in peers:
        pltpu.make_async_remote_copy(
            src_ref=fb, dst_ref=taps.at[mine], send_sem=f_send, recv_sem=f_recv.at[my_group],
            device_id=(peer, si), device_id_type=MESH).start()
    tail = pltpu.make_async_remote_copy(
        src_ref=mix.at[pl.ds(span - width, width)], dst_ref=halo, send_sem=tail_send, recv_sem=tail_recv,
        device_id=(fi, lax.rem(si + 1, ns)), device_id_type=MESH)

    @pl.when(si < ns - 1)
    def _():
        tail.start()

    def pack(first, block):
        for k in range(block.shape[1] // group):
            for h in range(parts):
                low, high = max(first, h * rows), min(first + block.shape[0], h * rows + width + rows)
                piece = block[low - first:high - first, k * group:(k + 1) * group]
                packed[k, low - h * rows:high - h * rows, h * group:(h + 1) * group] = piece

    pack(width, mix[...].astype(jnp.float32))
    load_q.wait()
    gate = qb[...].astype(jnp.float32)
    for k in range(groups):
        for h in range(parts):
            piece = gate[h * rows:(h + 1) * rows, k * group:(k + 1) * group]
            gates[k, :, h * group:(h + 1) * group] = piece

    @pl.when(si > 0)
    def _():
        tail.wait_recv()
        pack(0, halo[...].astype(jnp.float32))

    @pl.when(si == 0)
    def _():
        pack(0, jnp.zeros(halo.shape, jnp.float32))

    tiles = rows // SUB
    spread = width // SUB
    upper = (my_group * 2) // groups

    def one_group(order, carry):
        g = order + upper * (groups - 1 - 2 * order)
        block = taps.at[pl.ds(pl.multiple_of(g * group, group), group)]
        pltpu.make_async_copy(block, block, f_recv.at[g]).wait()
        tapsT[...] = jnp.concatenate([block[...]] * parts, axis=0).T
        acc = [[jnp.zeros((SUB, LANES), jnp.float32) for _ in range(tiles)] for _ in range(4)]
        for b in range(SUB):
            weights = [jnp.broadcast_to(tapsT[a * SUB + b:a * SUB + b + 1, :], (SUB, LANES)) for a in range(spread)]
            for row in range(1, spread + tiles):
                window = packed[g, row * SUB - b:row * SUB - b + SUB, :]
                for a in range(spread):
                    j = row - spread + a
                    if 0 <= j < tiles:
                        acc[a % 4][j] = acc[a % 4][j] + weights[a] * window
        total = jnp.concatenate([(p + q) + (r + s) for p, q, r, s in zip(*acc)], axis=0)
        done[g] = total * gates[g]
        return carry

    lax.fori_loop(0, groups, one_group, 0)

    for c in range(channels // LANES):
        for h in range(parts):
            pieces = [done[c * parts + k, :, h * group:(h + 1) * group] for k in range(parts)]
            out_ref[0, h * rows:(h + 1) * rows, c * LANES:(c + 1) * LANES] = (
                jnp.concatenate(pieces, axis=1).astype(jnp.bfloat16))

    others = taps.at[pl.ds(0, channels - own)]
    pltpu.make_async_copy(others, others, f_send).wait()

    @pl.when(si < ns - 1)
    def _():
        tail.wait_send()


def solution(mesh):
    nf, ns = mesh.shape["fsdp"], mesh.shape["seq"]

    def per_device(query_proj, key_proj, value_proj, filters):
        _, span, channels = key_proj.shape
        own, width = filters.shape
        group = max(own, 32)
        groups, rows = channels // group, span * group // LANES
        operands = [pltpu.with_memory_space_constraint(x, pltpu.HBM)
                    for x in (query_proj, key_proj, value_proj, filters)]
        return pl.pallas_call(
            functools.partial(kernel, nf, ns, group),
            out_shape=jax.ShapeDtypeStruct(query_proj.shape, jnp.bfloat16),
            in_specs=[pl.BlockSpec(memory_space=pltpu.HBM)] * 4,
            out_specs=pl.BlockSpec(memory_space=pltpu.VMEM),
            scratch_shapes=[
                pltpu.VMEM((span, channels), jnp.bfloat16),
                pltpu.VMEM((span, channels), jnp.bfloat16),
                pltpu.VMEM((span, channels), jnp.bfloat16),
                pltpu.VMEM((own, width), jnp.float32),
                pltpu.VMEM((span, channels), jnp.bfloat16),
                pltpu.VMEM((width, channels), jnp.bfloat16),
                pltpu.VMEM((channels, width), jnp.float32),
                pltpu.VMEM((width, LANES), jnp.float32),
                pltpu.VMEM((groups, width + rows, LANES), jnp.float32),
                pltpu.VMEM((groups, rows, LANES), jnp.float32),
                pltpu.VMEM((groups, rows, LANES), jnp.float32),
                pltpu.SemaphoreType.DMA((4,)),
                pltpu.SemaphoreType.DMA,
                pltpu.SemaphoreType.DMA,
                pltpu.SemaphoreType.DMA,
                pltpu.SemaphoreType.DMA((groups,)),
            ],
            compiler_params=pltpu.CompilerParams(collective_id=0, has_side_effects=True,
                                                 vmem_limit_bytes=40 * 1024 * 1024),
        )(*operands)

    in_specs = (P("fsdp", "seq", None),) * 3 + (P("fsdp", None),)
    return jax.shard_map(per_device, mesh=mesh, in_specs=in_specs, out_specs=P("fsdp", "seq", None), check_vma=False)
```

time: 9.77 us -> 9.45 us (0.967)
  Pallas kernels: 8.97 us -> 8.65 us
    pallas_call x1, Pallas kernels: 8.97 us -> 8.65 us  [per_device(): pl.pallas_call(functools.partial(kernel, nf, ns, group), out_shape=jax.Sh...]
where the time goes in v1:
time: 9.45 us; the launch traced here: 9.27 us
  Pallas kernels  8.65 us (92%)
  local copies, waits for them, and re-layouts  0.62 us (7%)
    pallas_call x1, Pallas kernels, per_device(): pl.pallas_call(functools.partial(kernel, nf, ns, group), out_shape=jax.Sh...  8.65 us
    unnamed x1, local copies, waits for them, and re-layouts  0.62 us

profile of v1, /device:TPU:0, one launch (start us, length us, event | category | flops | bytes accessed | tf_op | source)
XLA Modules:
  0.0 9.3 jit_solution(10256593663001141999)
XLA Ops:
  0.0 8.6 %shard_map.46 = bf16[1,128,128]{2,1,0:T(8,128)(2,1)S(1)} custom-call(bf16[1,128,128]{2,1,0:T(8,128)(2,1)} %q_hbm.1, bf16[1,128,128]{2,1,0:T(8,128)(2,1)} %k_hbm.1, bf16[1,128,128]{2,1,0:T(8,128)(2,1)} %v_hbm.1, f32[16,128]{1,0:T(8,128)} %f_hbm.1), custom_call_target="tpu_custom_call" | custom-call | tf_op jit(solution)/shard_map/pallas_call | solution.py:157
  8.7 0.6 %copy.6 = bf16[1,128,128]{2,1,0:T(8,128)(2,1)} copy(bf16[1,128,128]{2,1,0:T(8,128)(2,1)S(1)} %shard_map.46) | data formatting | bytes 65536

commit v2 on v1

--- a/solution.py
+++ b/solution.py
@@ -25,7 +25,7 @@
     return found
 
 
-def kernel(nf, ns, group, q_hbm, k_hbm, v_hbm, f_hbm, out_ref, kb, vb, qb, fb, mix, halo, taps, tapsT, packed, gates,
+def kernel(nf, ns, group, q_hbm, k_hbm, v_hbm, f_hbm, out_ref, kb, vb, qb, fb, mix, halo, taps, packed, gates,
            done, load_sem, tail_send, tail_recv, f_send, f_recv):
     fi = lax.axis_index("fsdp")
     si = lax.axis_index("seq")
@@ -70,10 +70,11 @@
     def _():
         pl.semaphore_wait(barrier, nf - 1)
 
-    for peer in peers:
+    for peer in peers[:4]:
         pltpu.make_async_remote_copy(
             src_ref=fb, dst_ref=taps.at[mine], send_sem=f_send, recv_sem=f_recv.at[my_group],
             device_id=(peer, si), device_id_type=MESH).start()
+
     tail = pltpu.make_async_remote_copy(
         src_ref=mix.at[pl.ds(span - width, width)], dst_ref=halo, send_sem=tail_send, recv_sem=tail_recv,
         device_id=(fi, lax.rem(si + 1, ns)), device_id_type=MESH)
@@ -81,6 +82,11 @@
     @pl.when(si < ns - 1)
     def _():
         tail.start()
+
+    for peer in peers[4:]:
+        pltpu.make_async_remote_copy(
+            src_ref=fb, dst_ref=taps.at[mine], send_sem=f_send, recv_sem=f_recv.at[my_group],
+            device_id=(peer, si), device_id_type=MESH).start()
 
     def pack(first, block):
         for k in range(block.shape[1] // group):
@@ -114,10 +120,10 @@
         g = order + upper * (groups - 1 - 2 * order)
         block = taps.at[pl.ds(pl.multiple_of(g * group, group), group)]
         pltpu.make_async_copy(block, block, f_recv.at[g]).wait()
-        tapsT[...] = jnp.concatenate([block[...]] * parts, axis=0).T
+        turned = jnp.concatenate([block[...]] * parts, axis=0).T
         acc = [[jnp.zeros((SUB, LANES), jnp.float32) for _ in range(tiles)] for _ in range(4)]
         for b in range(SUB):
-            weights = [jnp.broadcast_to(tapsT[a * SUB + b:a * SUB + b + 1, :], (SUB, LANES)) for a in range(spread)]
+            weights = [jnp.broadcast_to(turned[a * SUB + b:a * SUB + b + 1, :], (SUB, LANES)) for a in range(spread)]
             for row in range(1, spread + tiles):
                 window = packed[g, row * SUB - b:row * SUB - b + SUB, :]
                 for a in range(spread):
@@ -167,7 +173,6 @@
                 pltpu.VMEM((span, channels), jnp.bfloat16),
                 pltpu.VMEM((width, channels), jnp.bfloat16),
                 pltpu.VMEM((channels, width), jnp.float32),
-                pltpu.VMEM((width, LANES), jnp.float32),
                 pltpu.VMEM((groups, width + rows, LANES), jnp.float32),
                 pltpu.VMEM((groups, rows, LANES), jnp.float32),
                 pltpu.VMEM((groups, rows, LANES), jnp.float32),

time: 9.45 us -> 9.44 us (level)
  no operation moved by 1% of the time
where the time goes in v2:
time: 9.44 us; the launch traced here: 9.26 us
  Pallas kernels  8.63 us (91%)
  local copies, waits for them, and re-layouts  0.62 us (7%)
    pallas_call x1, Pallas kernels, per_device(): pl.pallas_call(functools.partial(kernel, nf, ns, group), out_shape=jax.Sh...  8.63 us
    unnamed x1, local copies, waits for them, and re-layouts  0.62 us

profile of v2, /device:TPU:0, one launch (start us, length us, event | category | flops | bytes accessed | tf_op | source)
XLA Modules:
  0.0 9.3 jit_solution(4033824930265486314)
XLA Ops:
  0.0 8.6 %shard_map.46 = bf16[1,128,128]{2,1,0:T(8,128)(2,1)S(1)} custom-call(bf16[1,128,128]{2,1,0:T(8,128)(2,1)} %q_hbm.1, bf16[1,128,128]{2,1,0:T(8,128)(2,1)} %k_hbm.1, bf16[1,128,128]{2,1,0:T(8,128)(2,1)} %v_hbm.1, f32[16,128]{1,0:T(8,128)} %f_hbm.1), custom_call_target="tpu_custom_call" | custom-call | tf_op jit(solution)/shard_map/pallas_call | solution.py:163
  8.6 0.6 %copy.6 = bf16[1,128,128]{2,1,0:T(8,128)(2,1)} copy(bf16[1,128,128]{2,1,0:T(8,128)(2,1)S(1)} %shard_map.46) | data formatting | bytes 65536
